TPU v7x, 128 devices: a whole 4x4x4 slice. The times are simulated.
128 devices in a mesh: seq: 8 (over z, x_hi), shard: 16 (over y, x_lo, core).
Axes of the slice: x: 4 (x_hi: 2, x_lo: 2; x = x_hi * 2 + x_lo), y: 4, z: 4, core: 2. Of those that a mesh axis runs over, the one named last changes fastest.
Arguments:
- tokens: bfloat16 [16, 1024, 1536], P('shard', 'seq'), may hold values from -6 to 6
- lengths: int32 [16], P('shard'), may hold values from 256 to 1024, as said below
- cotangent: bfloat16 [16, 1024, 1536], P('shard', 'seq'), may hold values from -6 to 6
- gain_one: bfloat16 [1536], P('shard'), may hold values from 0.099609375 to 1.8984375
- in_weight: bfloat16 [1536, 4608], P('shard'), may hold values from -0.15625 to 0.15625
- conv_weight: bfloat16 [3, 1536], P(None, 'shard'), may hold values from -3 to 3
- out_weight: bfloat16 [1536, 1536], P('shard'), may hold values from -0.15625 to 0.15625
- gain_two: bfloat16 [1536], P('shard'), may hold values from 0.099609375 to 1.8984375
- gate_weight: bfloat16 [1536, 6912], P('shard'), may hold values from -0.15625 to 0.15625
- up_weight: bfloat16 [1536, 6912], P('shard'), may hold values from -0.15625 to 0.15625
- down_weight: bfloat16 [6912, 1536], P('shard'), may hold values from -0.078125 to 0.078125
Outputs:
- output: bfloat16 [16, 1024, 1536], P('shard', 'seq')
- grad_tokens: float32 [16, 1024, 1536], P('shard', 'seq')
- grad_gain_one: float32 [1536], P('shard')
- grad_in_weight: float32 [1536, 4608], P('shard')
- grad_conv_weight: float32 [3, 1536], P(None, 'shard')
- grad_out_weight: float32 [1536, 1536], P('shard')
- grad_gain_two: float32 [1536], P('shard')
- grad_gate_weight: float32 [1536, 6912], P('shard')
- grad_up_weight: float32 [1536, 6912], P('shard')
- grad_down_weight: float32 [6912, 1536], P('shard')
Inputs may be any that keep to these rules, and one draw needn't show every extreme that they name: `lengths`: in each aligned pair of sequences (0 and 1, 2 and 3, and so on) one, drawn from the seed, has length 1024.
All inputs are finite; a program needn't handle non-finite values.
Results may differ from a plain program's by a relative error of at most 0.022.
Values may be sent and summed in bfloat16 or wider, within the bound.
No kernel may reach another device: no remote copies, remote signals or barrier semaphores. Data moves between devices by JAX's collectives and lax.ppermute only.
A program may use at most 320 MiB of HBM per device.

v0:
```python
import jax
import jax.numpy as jnp
from jax import lax
from jax.sharding import PartitionSpec as P

epsilon = 1e-05


def from_behind(block, axis, distance):
    devices = range(lax.axis_size(axis))
    route = [(i - distance, i) for i in devices if i - distance in devices]
    return lax.ppermute(block, axis, route)


def matmul(left, right):
    return jnp.dot(left, right, preferred_element_type=jnp.float32)


def matmul_right_t(left, right):
    return lax.dot_general(
        left, right, (((1,), (1,)), ((), ())), preferred_element_type=jnp.float32
    )


def matmul_left_t(left, right):
    return lax.dot_general(
        left, right, (((0,), (0,)), ((), ())), preferred_element_type=jnp.float32
    )


def normalize(value_rows, gain):
    scale = lax.rsqrt(jnp.mean(value_rows * value_rows, axis=-1, keepdims=True) + epsilon)
    base = value_rows * scale
    return (base, scale, (base * gain).astype(jnp.bfloat16))


def norm_back(gradient_normalized, base, scale, gain):
    grad_gain = jnp.sum(gradient_normalized * base, axis=0)
    grad_base = gradient_normalized * gain
    grad_values = scale * (grad_base - base * jnp.mean(grad_base * base, axis=-1, keepdims=True))
    return (grad_values, grad_gain)


def conv_forward(gated_in, kernel):
    seq_rows = gated_in.shape[1]
    earlier = from_behind(gated_in[:, seq_rows - 2 :], "seq", 1)
    extended = jnp.concatenate([earlier, gated_in], axis=1)
    conv_out = (
        kernel[0] * extended[:, :seq_rows]
        + kernel[1] * extended[:, 1 : seq_rows + 1]
        + kernel[2] * extended[:, 2:]
    )
    return (extended, conv_out)


def conv_backward(grad_conv, extended, kernel):
    seq_rows = grad_conv.shape[1]
    grad_extended = jnp.pad(kernel[0] * grad_conv, ((0, 0), (0, 2), (0, 0)))
    grad_extended = grad_extended + jnp.pad(kernel[1] * grad_conv, ((0, 0), (1, 1), (0, 0)))
    grad_extended = grad_extended + jnp.pad(kernel[2] * grad_conv, ((0, 0), (2, 0), (0, 0)))
    grad_kernel = jnp.stack(
        [
            jnp.sum(grad_conv * extended[:, offset : offset + seq_rows], axis=(0, 1))
            for offset in range(3)
        ]
    )
    returned = from_behind(grad_extended[:, :2], "seq", -1)
    grad_gated_in = grad_extended[:, 2:] + jnp.pad(returned, ((0, 0), (seq_rows - 2, 0), (0, 0)))
    return (grad_gated_in, grad_kernel)


def local(
    tokens,
    lengths,
    cotangent,
    gain_one,
    in_weight,
    conv_weight,
    out_weight,
    gain_two,
    gate_weight,
    up_weight,
    down_weight,
):
    seqs_here, seq_rows, width = tokens.shape
    total_rows = seqs_here * seq_rows
    position = lax.axis_index("seq") * seq_rows + jnp.arange(seq_rows, dtype=jnp.int32)
    valid_rows = (position[None, :] < lengths[:, None]).astype(jnp.float32).reshape(total_rows, 1)
    hidden = tokens.astype(jnp.float32).reshape(total_rows, width)
    grad_result = valid_rows * cotangent.astype(jnp.float32).reshape(total_rows, width)
    grad_branch = grad_result.astype(jnp.bfloat16)
    gathered = (
        lax.all_gather(gain_one, "shard", axis=0, tiled=True),
        lax.all_gather(in_weight, "shard", axis=0, tiled=True),
        lax.all_gather(conv_weight, "shard", axis=1, tiled=True),
        lax.all_gather(out_weight, "shard", axis=0, tiled=True),
        lax.all_gather(gain_two, "shard", axis=0, tiled=True),
        lax.all_gather(gate_weight, "shard", axis=0, tiled=True),
        lax.all_gather(up_weight, "shard", axis=0, tiled=True),
        lax.all_gather(down_weight, "shard", axis=0, tiled=True),
    )
    gain_first = gathered[0].astype(jnp.float32)
    base_one, scale_one, normed = normalize(hidden, gain_first)
    triple = matmul(normed, gathered[1])
    input_gate = triple[:, :width]
    output_gate = triple[:, width : 2 * width]
    conv_values = triple[:, 2 * width :]
    gated_in = (input_gate * conv_values).reshape(seqs_here, seq_rows, width)
    kernel = gathered[2].astype(jnp.float32)
    extended, conv_out = conv_forward(gated_in, kernel)
    conv_out = conv_out.reshape(total_rows, width)
    mixed = (output_gate * conv_out).astype(jnp.bfloat16)
    middle = hidden + matmul(mixed, gathered[3])
    gain_second = gathered[4].astype(jnp.float32)
    base_two, scale_second, normed_two = normalize(middle, gain_second)
    gate_pre = matmul(normed_two, gathered[5])
    up_pre = matmul(normed_two, gathered[6])
    sigmoid_gate = jax.nn.sigmoid(gate_pre)
    silu_gate = gate_pre * sigmoid_gate
    active = (silu_gate * up_pre).astype(jnp.bfloat16)
    result = valid_rows * (middle + matmul(active, gathered[7]))
    weights = (
        lax.all_gather(gain_one, "shard", axis=0, tiled=True),
        lax.all_gather(in_weight, "shard", axis=0, tiled=True),
        lax.all_gather(conv_weight, "shard", axis=1, tiled=True),
        lax.all_gather(out_weight, "shard", axis=0, tiled=True),
        lax.all_gather(gain_two, "shard", axis=0, tiled=True),
        lax.all_gather(gate_weight, "shard", axis=0, tiled=True),
        lax.all_gather(up_weight, "shard", axis=0, tiled=True),
        lax.all_gather(down_weight, "shard", axis=0, tiled=True),
    )
    grad_down_w = matmul_left_t(active, grad_branch)
    grad_active = matmul_right_t(grad_branch, weights[7])
    grad_gate = (
        grad_active * up_pre * sigmoid_gate * (1.0 + gate_pre * (1.0 - sigmoid_gate))
    ).astype(jnp.bfloat16)
    grad_up = (grad_active * silu_gate).astype(jnp.bfloat16)
    grad_gate_w = matmul_left_t(normed_two, grad_gate)
    grad_up_w = matmul_left_t(normed_two, grad_up)
    grad_normed_two = matmul_right_t(grad_gate, weights[5]) + matmul_right_t(grad_up, weights[6])
    grad_mid_norm, grad_gain_two = norm_back(grad_normed_two, base_two, scale_second, gain_second)
    ffn_part = (
        lax.psum_scatter(
            grad_gain_two.astype(jnp.bfloat16), "shard", scatter_dimension=0, tiled=True
        ).astype(jnp.float32),
        lax.psum_scatter(
            grad_gate_w.astype(jnp.bfloat16), "shard", scatter_dimension=0, tiled=True
        ).astype(jnp.float32),
        lax.psum_scatter(
            grad_up_w.astype(jnp.bfloat16), "shard", scatter_dimension=0, tiled=True
        ).astype(jnp.float32),
        lax.psum_scatter(
            grad_down_w.astype(jnp.bfloat16), "shard", scatter_dimension=0, tiled=True
        ).astype(jnp.float32),
    )
    grad_middle = grad_result + grad_mid_norm
    grad_mixer = grad_middle.astype(jnp.bfloat16)
    grad_out_w = matmul_left_t(mixed, grad_mixer)
    grad_mixed = matmul_right_t(grad_mixer, weights[3])
    grad_output_gate = grad_mixed * conv_out
    grad_conv = (grad_mixed * output_gate).reshape(seqs_here, seq_rows, width)
    grad_gated_in, grad_kernel = conv_backward(grad_conv, extended, kernel)
    grad_gated_in = grad_gated_in.reshape(total_rows, width)
    grad_triple = jnp.concatenate(
        [grad_gated_in * conv_values, grad_output_gate, grad_gated_in * input_gate], axis=1
    ).astype(jnp.bfloat16)
    grad_in_w = matmul_left_t(normed, grad_triple)
    gradient_normalized = matmul_right_t(grad_triple, weights[1])
    grad_hidden_norm, grad_gain_one = norm_back(
        gradient_normalized, base_one, scale_one, gain_first
    )
    grad_tokens = (grad_middle + grad_hidden_norm).reshape(tokens.shape)
    mixer_part = (
        lax.psum_scatter(
            grad_gain_one.astype(jnp.bfloat16), "shard", scatter_dimension=0, tiled=True
        ).astype(jnp.float32),
        lax.psum_scatter(
            grad_in_w.astype(jnp.bfloat16), "shard", scatter_dimension=0, tiled=True
        ).astype(jnp.float32),
        lax.psum_scatter(
            grad_kernel.astype(jnp.bfloat16), "shard", scatter_dimension=1, tiled=True
        ).astype(jnp.float32),
        lax.psum_scatter(
            grad_out_w.astype(jnp.bfloat16), "shard", scatter_dimension=0, tiled=True
        ).astype(jnp.float32),
    )
    portion_list = (
        mixer_part[0],
        mixer_part[1],
        mixer_part[2],
        mixer_part[3],
        ffn_part[0],
        ffn_part[1],
        ffn_part[2],
        ffn_part[3],
    )
    output = result.astype(jnp.bfloat16).reshape(tokens.shape)
    summed = (
        lax.psum(portion_list[0].astype(jnp.bfloat16), "seq").astype(jnp.float32),
        lax.psum(portion_list[1].astype(jnp.bfloat16), "seq").astype(jnp.float32),
        lax.psum(portion_list[2].astype(jnp.bfloat16), "seq").astype(jnp.float32),
        lax.psum(portion_list[3].astype(jnp.bfloat16), "seq").astype(jnp.float32),
        lax.psum(portion_list[4].astype(jnp.bfloat16), "seq").astype(jnp.float32),
        lax.psum(portion_list[5].astype(jnp.bfloat16), "seq").astype(jnp.float32),
        lax.psum(portion_list[6].astype(jnp.bfloat16), "seq").astype(jnp.float32),
        lax.psum(portion_list[7].astype(jnp.bfloat16), "seq").astype(jnp.float32),
    )
    return (
        output,
        grad_tokens,
        summed[0],
        summed[1],
        summed[2],
        summed[3],
        summed[4],
        summed[5],
        summed[6],
        summed[7],
    )


def solution(mesh):
    placed = (
        P("shard", "seq", None),
        P("shard"),
        P("shard", "seq", None),
        P("shard"),
        P("shard", None),
        P(None, "shard"),
        P("shard", None),
        P("shard"),
        P("shard", None),
        P("shard", None),
        P("shard", None),
    )
    return jax.shard_map(
        local,
        mesh=mesh,
        in_specs=placed,
        out_specs=(
            P("shard", "seq", None),
            P("shard", "seq", None),
            P("shard"),
            P("shard", None),
            P(None, "shard"),
            P("shard", None),
            P("shard"),
            P("shard", None),
            P("shard", None),
            P("shard", None),
        ),
        check_vma=False,
    )
```

profile of v0, /device:TPU:1, one launch (start us, length us, event | category | flops | bytes accessed | tf_op | source)
XLA Modules:
  0.0 1741.7 jit_solution(5554776693987444049)
XLA Ops:
  13.1 29.8 %all-reduce.9 = (bf16[1536]{0:T(1024)(128)(2,1)S(1)}, bf16[1536]{0:T(1024)(128)(2,1)}) all-reduce(bf16[1536]{0:T(1024)(128)(2,1)S(1)} %dynamic-update-slice, bf16[1536]{0:T(1024)(128)(2,1)S(1)} %dynamic-update-slice.1), channel_id=1, replica_groups=mesh['seq'=8,'shard'=16] {'shard'}, use_global_device_ids=true, to_apply=%add.4 | all-reduce | flops 3072 | bytes 12288
  42.9 19.9 %all-gather = bf16[16,96,3]{1,2,0:T(4,128)(2,1)S(1)} all-gather(bf16[1,96,3]{1,2,0:T(4,128)(2,1)S(1)} %bitcast.90), channel_id=1, replica_groups=mesh['seq'=8,'shard'=16] {'shard'}, dimensions={0}, use_global_device_ids=true | all-gather | bytes 9792 | tf_op jit(solution)/shard_map/all_gather | solution.py:95
  63.8 29.9 %all-gather.7.cloned.1.call-done = bf16[1536,4608]{1,0:T(8,128)(2,1)} async-done(((bf16[96,4608]{1,0:T(8,128)(2,1)}), bf16[1536,4608]{1,0:T(8,128)(2,1)}) %all-gather.7.cloned.1.call-update) | async-done | bytes 14155792 | tf_op jit(solution)/shard_map/all_gather | solution.py:94
  93.7 7.1 fusion.32
  100.9 4.3 collective-permute-start
  106.7 1.3 fusion.22
  108.0 26.7 %all-gather.9.cloned.1.call-done = bf16[1536,1536]{1,0:T(8,128)(2,1)} async-done(((bf16[96,1536]{1,0:T(8,128)(2,1)}), bf16[1536,1536]{1,0:T(8,128)(2,1)}) %all-gather.9.cloned.1.call-update) | async-done | bytes 4718608 | tf_op jit(solution)/shard_map/all_gather | solution.py:96
  134.7 3.3 multiply_reduce_fusion.3
  138.6 0.9 multiply_convert_fusion.5
  139.5 109.7 %all-gather.13.cloned.1.call-done = bf16[1536,6912]{1,0:T(8,128)(2,1)} async-done(((bf16[96,6912]{1,0:T(8,128)(2,1)}), bf16[1536,6912]{1,0:T(8,128)(2,1)}) %all-gather.13.cloned.1.call-update) | async-done | bytes 21233680 | tf_op jit(solution)/shard_map/all_gather | solution.py:99
  249.2 11.9 fusion.39
  261.0 103.3 %all-gather.11.cloned.1.call-done = bf16[1536,6912]{1,0:T(8,128)(2,1)} async-done(((bf16[96,6912]{1,0:T(8,128)(2,1)}), bf16[1536,6912]{1,0:T(8,128)(2,1)}) %all-gather.11.cloned.1.call-update) | async-done | bytes 21233680 | tf_op jit(solution)/shard_map/all_gather | solution.py:98
  364.3 11.9 fusion.38
  376.2 103.2 %all-gather.15.cloned.1.call-done = bf16[6912,1536]{1,0:T(8,128)(2,1)} async-done(((bf16[432,1536]{1,0:T(8,128)(2,1)}), bf16[6912,1536]{1,0:T(8,128)(2,1)}) %all-gather.15.cloned.1.call-update) | async-done | bytes 21233680 | tf_op jit(solution)/shard_map/all_gather | solution.py:100
  479.4 14.6 multiply_convert_fusion
  494.0 11.6 fusion.40
  505.7 12.0 multiply_reduce_fusion
  518.1 0.9 copy-done.3
  518.9 3.5 convolution_convert_fusion.4
  522.6 5.4 fusion.20
  528.3 1.3 collective-permute-start.1
  529.9 4.3 collective-permute-done.1
  535.5 7.3 convolution_convert_fusion.3
  542.8 1.4 copy-done.5
  544.3 10.4 convolution_convert_fusion
  554.8 1.4 copy-done.2
  556.3 10.2 convolution_convert_fusion.1
  566.6 1.4 copy-done
  568.0 10.3 convolution_convert_fusion.2
  579.0 1.0 copy.24
  580.3 11.4 reduce-scatter.11.cloned.1.call-done
  591.7 158.4 %reduce-scatter.9.cloned.1.call-done = bf16[96,4608]{1,0:T(8,128)(2,1)} async-done(((bf16[1536,4608]{1,0:T(8,128)(2,1)}), bf16[96,4608]{1,0:T(8,128)(2,1)}) %reduce-scatter.9.cloned.1.call-update) | async-done | bytes 884752 | tf_op jit(solution)/shard_map/reduce_scatter | solution.py:177
  750.1 228.5 %reduce-scatter.17.cloned.1.call-done = bf16[432,1536]{1,0:T(8,128)(2,1)} async-done(((bf16[6912,1536]{1,0:T(8,128)(2,1)}), bf16[432,1536]{1,0:T(8,128)(2,1)}) %reduce-scatter.17.cloned.1.call-update) | async-done | bytes 1327120 | tf_op jit(solution)/shard_map/reduce_scatter | solution.py:152
  978.6 228.6 %reduce-scatter.15.cloned.1.call-done = bf16[96,6912]{1,0:T(8,128)(2,1)} async-done(((bf16[1536,6912]{1,0:T(8,128)(2,1)}), bf16[96,6912]{1,0:T(8,128)(2,1)}) %reduce-scatter.15.cloned.1.call-update) | async-done | bytes 1327120 | tf_op jit(solution)/shard_map/reduce_scatter | solution.py:149
  1207.2 228.3 %reduce-scatter.13.cloned.1.call-done = bf16[96,6912]{1,0:T(8,128)(2,1)} async-done(((bf16[1536,6912]{1,0:T(8,128)(2,1)}), bf16[96,6912]{1,0:T(8,128)(2,1)}) %reduce-scatter.13.cloned.1.call-update) | async-done | bytes 1327120 | tf_op jit(solution)/shard_map/reduce_scatter | solution.py:146
  1436.3 10.8 fusion.3
  1447.1 9.8 fusion.15
  1456.9 29.4 %all-reduce.8 = (bf16[1536]{0:T(1024)(128)(2,1)S(1)}, bf16[1536]{0:T(1024)(128)(2,1)S(1)}) all-reduce(bf16[1536]{0:T(1024)(128)(2,1)S(1)} %get-tuple-element.14, bf16[1536]{0:T(1024)(128)(2,1)S(1)} %copy-done.32), channel_id=2, replica_groups=mesh['seq'=8,'shard'=16] {'shard'}, use_global_device_ids=true, to_apply=%region_5.0.clone | all-reduce | flops 3072 | bytes 12288
  1486.5 1.2 fusion.14
  1487.7 8.4 reduce-scatter.19.cloned.1.call-done
  1496.0 0.8 copy.25
  1496.8 21.0 %all-reduce.10 = (bf16[96]{0:T(256)(128)(2,1)S(1)}, bf16[3,96]{1,0:T(4,128)(2,1)S(1)}, bf16[96]{0:T(256)(128)(2,1)S(1)}) all-reduce(bf16[96]{0:T(256)(128)(2,1)S(1)} %dynamic-slice.3, bf16[3,96]{1,0:T(4,128)(2,1)S(1)} %copy.25, bf16[96]{0:T(256)(128)(2,1)S(1)} %dynamic-slice.5), channel_id=1, replica_groups=mesh['seq'=8,'shard'=16] {'seq'}, use_global_device_ids=true, to_apply=%region_6.0 | all-reduce | flops 480 | bytes 1920 | tf_op jit(solution)/shard_map/psum | solution.py:199
  1519.4 205.3 %all-reduce.14.cloned.1.call-done = (bf16[96,4608]{1,0:T(8,128)(2,1)}, bf16[96,1536]{1,0:T(8,128)(2,1)}, bf16[96,6912]{1,0:T(8,128)(2,1)}, bf16[96,6912]{1,0:T(8,128)(2,1)}, bf16[432,1536]{1,0:T(8,128)(2,1)}) async-done(((bf16[96,4608]{1,0:T(8,128)(2,1)}, bf16[96,1536]{1,0:T(8,128)(2,1)}, bf16[96,6912]{1,0:T(8,128)(2,1)}, bf16[96,6912]{1,0:T(8,128)(2,1)}, bf16[432,1536]{1,0:T(8,128)(2,1)}), ...) | async-done | bytes 5160976 | tf_op jit(solution)/shard_map/psum | solution.py:200
  1724.7 1.9 convert_element_type.137
  1726.6 2.6 convert_element_type.134
  1729.3 1.7 convert_element_type.141
  1730.9 1.7 convert_element_type.143
  1732.6 1.8 convert_element_type.145
  (142 shorter events, 12.8 us)
Async XLA Ops:
  7.2 4.1 copy-start.40
  7.2 5.4 copy-start.42
  7.2 5.6 copy-start.43
  7.2 35.7 %copy-start.41 = (bf16[3,96]{1,0:T(4,128)(2,1)S(1)}, bf16[3,96]{1,0:T(4,128)(2,1)}, u32[]{:S(2)}) copy-start(bf16[3,96]{1,0:T(4,128)(2,1)} %param.16) | copy-start | bytes 1732
  7.2 56.4 %copy-start.7 = (bf16[1,128,1536]{2,1,0:T(8,128)(2,1)S(1)}, bf16[1,128,1536]{2,1,0:T(8,128)(2,1)}, u32[]{:S(2)}) copy-start(bf16[1,128,1536]{2,1,0:T(8,128)(2,1)} %param.11) | copy-start | bytes 1179652
  7.2 86.4 %all-gather.7.cloned.1.call-start = ((), (), s32[]{:S(2)}) async-start(), calls=%async_computation.6 | async-start | bytes 15040512 | tf_op jit(solution)/shard_map/all_gather | solution.py:94
  8.0 126.8 %all-gather.9.cloned.1.call-start = ((), (), s32[]{:S(2)}) async-start(), calls=%async_computation.7 | async-start | bytes 5013504 | tf_op jit(solution)/shard_map/all_gather | solution.py:96
  8.7 240.4 %all-gather.13.cloned.1.call-start = ((), (), s32[]{:S(2)}) async-start(), calls=%async_computation.9 | async-start | bytes 22560768 | tf_op jit(solution)/shard_map/all_gather | solution.py:99
  9.4 354.9 %all-gather.11.cloned.1.call-start = ((), (), s32[]{:S(2)}) async-start(), calls=%async_computation.8 | async-start | bytes 22560768 | tf_op jit(solution)/shard_map/all_gather | solution.py:98
  10.0 469.4 %all-gather.15.cloned.1.call-start = ((), (), s32[]{:S(2)}) async-start(), calls=%async_computation.10 | async-start | bytes 22560768 | tf_op jit(solution)/shard_map/all_gather | solution.py:100
  10.6 581.1 %reduce-scatter.11.cloned.1.call-start = ((), (), s32[]{:S(2)}) async-start(), calls=%async_computation.12 | async-start | bytes 5013504 | tf_op jit(solution)/shard_map/reduce_scatter | solution.py:183
  63.8 29.9 %copy-start.33 = (f32[128]{0:T(128)}, f32[128]{0:T(128)S(1)}, u32[]{:S(2)}) copy-start(f32[128]{0:T(128)S(1)} %add_rsqrt_fusion.1) | copy-start | bytes 1540
  93.6 12.1 copy-start.39
  93.6 13.0 copy-start.23
  93.6 13.0 copy-start.25
  93.6 13.0 copy-start.27
  100.9 33.8 %copy-start.9 = (f32[1,128,1536]{2,1,0:T(8,128)}, f32[1,128,1536]{2,1,0:T(8,128)S(1)}, u32[]{:S(2)}) copy-start(f32[1,128,1536]{2,1,0:T(8,128)S(1)} %fusion.36) | copy-start | bytes 2359300
  100.9 5.1 collective-permute-start
  494.0 11.7 copy-start.1
  494.0 11.7 copy-start.38
  505.7 12.1 copy-start.12
  505.7 12.1 copy-start.35
  505.7 13.2 copy-start.10
  522.5 5.5 copy-start.24
  522.5 227.6 %reduce-scatter.9.cloned.1.call-start = ((), (), s32[]{:S(2)}) async-start(), calls=%async_computation.11 | async-start | bytes 15040512 | tf_op jit(solution)/shard_map/reduce_scatter | solution.py:177
  522.5 5.4 copy-start.26
  522.6 5.4 copy-start.28
  528.0 1.6 copy-start.11
  528.3 5.9 collective-permute-start.1
  529.7 4.9 copy-start.14
  529.7 5.8 copy-start.34
  542.8 1.5 copy-start.13
  542.8 1.6 copy-start.36
  542.8 435.8 %reduce-scatter.17.cloned.1.call-start = ((), (), s32[]{:S(2)}) async-start(), calls=%async_computation.15 | async-start | bytes 22560768 | tf_op jit(solution)/shard_map/reduce_scatter | solution.py:152
  554.7 1.5 copy-start.8
  554.7 652.5 %reduce-scatter.15.cloned.1.call-start = ((), (), s32[]{:S(2)}) async-start(), calls=%async_computation.14 | async-start | bytes 22560768 | tf_op jit(solution)/shard_map/reduce_scatter | solution.py:149
  566.5 869.0 %reduce-scatter.13.cloned.1.call-start = ((), (), s32[]{:S(2)}) async-start(), calls=%async_computation.13 | async-start | bytes 22560768 | tf_op jit(solution)/shard_map/reduce_scatter | solution.py:146
  578.3 858.0 %copy-start.6 = (bf16[128,6912]{1,0:T(8,128)(2,1)S(1)}, bf16[128,6912]{1,0:T(8,128)(2,1)}, u32[]{:S(2)}) copy-start(bf16[128,6912]{1,0:T(8,128)(2,1)} %get-tuple-element.36) | copy-start | bytes 5308420
  578.3 917.8 %reduce-scatter.19.cloned.1.call-start = ((), (), s32[]{:S(2)}) async-start(), calls=%async_computation.16 | async-start | bytes 417792
  580.0 1144.7 %all-reduce.14.cloned.1.call-start = ((), (), s32[]{:S(2)}) async-start(), calls=%async_computation.17 | async-start | bytes 10321920 | tf_op jit(solution)/shard_map/psum | solution.py:200
  1436.2 10.8 copy-start.15
  1436.2 10.8 copy-start.17
  1436.2 10.8 copy-start.19
  1447.1 9.9 copy-start.32
  1447.1 39.4 %copy-start.4 = (f32[128,1536]{1,0:T(8,128)S(1)}, f32[128,1536]{1,0:T(8,128)}, u32[]{:S(2)}) copy-start(f32[128,1536]{1,0:T(8,128)} %copy-done.3) | copy-start | bytes 2359300
  1724.7 4.6 copy-start.22
  1726.6 4.3 copy-start.21
  1729.3 3.4 copy-start.20
  (10 other events, 9.5 us)
Sparse Core Ops, SparseCore 0:
  9.8 83.8 all-gather.6
  95.3 39.3 all-gather.8
  136.4 112.6 all-gather.12
  250.7 113.5 all-gather.10
  365.9 113.5 all-gather.14
  522.6 69.0 reduce-scatter.10
  594.1 155.8 reduce-scatter.8
  752.5 226.0 reduce-scatter.16
  981.2 226.0 reduce-scatter.14
  1209.5 226.0 reduce-scatter.12
  1438.6 57.3 reduce-scatter.18
  1498.8 225.8 all-reduce.13
where the time goes:
time: 1750 us; the launch traced here: 1740 us
  waiting for transfers between devices  1450 us (83%)
  matrix products  140 us (8%)
  blocking collectives  100 us (6%)
    reduce_scatter x1, waiting for transfers between devices, local(): lax.psum_scatter(grad_up_w.astype(jnp.bfloat16), 'shard', scatter_dimensi...  229 us
    reduce_scatter x1, waiting for transfers between devices, local(): lax.psum_scatter(grad_down_w.astype(jnp.bfloat16), 'shard', scatter_dimen...  229 us
    reduce_scatter x1, waiting for transfers between devices, local(): lax.psum_scatter(grad_gate_w.astype(jnp.bfloat16), 'shard', scatter_dimen...  228 us
    psum x1, waiting for transfers between devices, local(): lax.psum(portion_list[1].astype(jnp.bfloat16), 'seq').astype(jnp.float32)  205 us
    reduce_scatter x1, waiting for transfers between devices, local(): lax.psum_scatter(grad_in_w.astype(jnp.bfloat16), 'shard', scatter_dimensi...  158 us
    all_gather x1, waiting for transfers between devices, local(): lax.all_gather(up_weight, 'shard', axis=0, tiled=True)  110 us
    all_gather x1, waiting for transfers between devices, local(): lax.all_gather(gate_weight, 'shard', axis=0, tiled=True)  103 us
    all_gather x1, waiting for transfers between devices, local(): lax.all_gather(down_weight, 'shard', axis=0, tiled=True)  103 us
  transfers between devices with their start and end apart: 14, of which 14 were waited for; matrix products, arithmetic and copies ran while one was open for 6% of the time, Pallas kernels for 0%

commit v1 on v0

v1 whole, which is shorter than its diff:
```python
import jax
import jax.numpy as jnp
from jax import lax
from jax.experimental import pallas as pl
from jax.experimental.pallas import tpu as pltpu
from jax.sharding import Mesh
from jax.sharding import PartitionSpec as P

epsilon = 1e-05
bf16 = jnp.bfloat16
f32 = jnp.float32
ring = ("xh", "xl")
owners = ("y", "xl", "core")
blocks = ("z", "xh")
lane = 128


def shift(value, axis, distance):
    if distance == 0:
        return value
    size = lax.axis_size(axis)
    return lax.ppermute(value, axis, [(i, (i + distance) % size) for i in range(size)])


def matmul(left, right):
    return jnp.dot(left, right, preferred_element_type=f32)


def matmul_right_t(left, right):
    return lax.dot_general(left, right, (((1,), (1,)), ((), ())), preferred_element_type=f32)


def matmul_left_t(left, right):
    return lax.dot_general(left, right, (((0,), (0,)), ((), ())), preferred_element_type=f32)


def gather_z(value):
    return [value] + [shift(value, "z", distance) for distance in (1, 2, 3)]


def scatter_z(parts):
    total = parts[0].astype(f32)
    for distance in (1, 2, 3):
        total = total + shift(parts[distance].astype(bf16), "z", -distance).astype(f32)
    return total


def in_order(parts, axis):
    place = lax.axis_index(axis)
    stacked = jnp.stack(parts)
    return [lax.dynamic_index_in_dim(stacked, (place - i) % 4, axis=0, keepdims=False) for i in range(4)]


def spread_rows(rows, direct=False):
    if direct:
        own = jnp.concatenate(in_order([rows] + [shift(rows, "y", d) for d in (1, 2, 3)], "y"), axis=0)
    else:
        own = lax.all_gather(rows, "y", axis=0, tiled=True)
    half = own.shape[0] // 2
    above = shift(own[:half], ring, 1)
    below = shift(own[half:], ring, -1)
    this_core = jnp.concatenate([own, above, below], axis=0)
    return this_core, shift(this_core, "core", 1)


def combine_rows(left, right, extra=None):
    width = left.shape[1]
    half, quarter = width // 2, width // 4

    def product(start, stop):
        out = matmul_left_t(left[:, start:stop], right)
        if extra is not None:
            out = out + jnp.pad(extra[start:stop], ((0, 0), (right.shape[1] - extra.shape[1], 0)))
        return out

    other_core = product(half, width).astype(bf16)
    arrived = shift(other_core, "core", 1)
    other_x = (product(quarter, half) + arrived[quarter:].astype(f32)).astype(bf16)
    cut = quarter // 2
    above = shift(other_x[:cut], ring, 1)
    below = shift(other_x[cut:], ring, -1)
    mine = product(0, quarter) + arrived[:quarter].astype(f32)
    mine = (mine + jnp.concatenate([above, below], axis=0).astype(f32)).astype(bf16)
    mine = lax.psum_scatter(mine, "y", scatter_dimension=0, tiled=True)
    return add_partner(mine)


def add_partner(mine):
    return (mine.astype(f32) + shift(mine, "xh", 1).astype(f32)).astype(bf16)


def normalize(value_rows, gain):
    scale = lax.rsqrt(jnp.mean(value_rows * value_rows, axis=-1, keepdims=True) + epsilon)
    base = value_rows * scale
    return (base, scale, (base * gain).astype(bf16))


def norm_back(gradient_normalized, base, scale, gain):
    grad_base = gradient_normalized * gain
    return scale * (grad_base - base * jnp.mean(grad_base * base, axis=-1, keepdims=True))


def place_rows(pieces, starts, total):
    rows, width = pieces[0].shape
    gap = total - rows * len(pieces)

    def body(starts_ref, *refs):
        sources, target, sems = refs[: len(pieces)], refs[-2], refs[-1]
        copies = []
        for i, source in enumerate(sources):
            at = pl.ds(pl.multiple_of(starts_ref[i], 16), rows)
            copies.append(pltpu.make_async_copy(source, target.at[at], sems.at[i]))
        for copy in copies:
            copy.start()
        blank = pl.multiple_of(starts_ref[len(pieces)], 16)
        target[pl.ds(blank, gap), :] = jnp.zeros((gap, width), target.dtype)
        for copy in copies:
            copy.wait()

    return pl.pallas_call(
        body,
        out_shape=jax.ShapeDtypeStruct((total, width), pieces[0].dtype),
        in_specs=[pl.BlockSpec(memory_space=pltpu.SMEM)] + [pl.BlockSpec(memory_space=pl.ANY)] * len(pieces),
        out_specs=pl.BlockSpec(memory_space=pltpu.VMEM),
        scratch_shapes=[pltpu.SemaphoreType.DMA((len(pieces),))],
        compiler_params=pltpu.CompilerParams(vmem_limit_bytes=32 * 1024 * 1024),
    )(starts, *pieces)


def local(
    tokens,
    lengths,
    cotangent,
    gain_one,
    in_weight,
    conv_weight,
    out_weight,
    gain_two,
    gate_weight,
    up_weight,
    down_weight,
):
    rows, width = tokens.shape[1:]
    z, xh, xl, core = (lax.axis_index(name) for name in ("z", "xh", "xl", "core"))
    y = lax.axis_index("y")
    own_rows = width // 16
    part = width // 4
    hidden_rows = down_weight.shape[0]
    hidden = 4 * hidden_rows
    padded = -(-hidden // lane) * lane
    gap = padded - hidden
    odd = z % 2

    position = (z * 2 + xh) * rows + jnp.arange(rows, dtype=jnp.int32)
    valid = (position < lengths[0]).astype(f32)[:, None]
    tokens_here = tokens[0]
    value_here = tokens_here.astype(f32)
    grad_result = valid * cotangent[0].astype(f32)
    grad_branch = grad_result.astype(bf16)

    index = jnp.arange(width, dtype=jnp.int32)
    row, piece = index % own_rows, index // own_rows
    source = (((piece % 4) * 2 + ((piece // 4) % 2 ^ xl)) * 2 + (piece // 8 ^ core)) * own_rows + row
    order = (index[:, None] == source[None, :]).astype(bf16)
    channel = (index + z * part) % width
    channel_order = (channel[:, None] == source[None, :]).astype(bf16)

    def to_rows(values):
        return matmul(values, order).astype(bf16)

    def from_rows(values):
        high = values.astype(bf16)
        low = (values - high.astype(f32)).astype(bf16)
        both = matmul_right_t(jnp.concatenate([high, low], axis=0), order)
        return both[:rows] + both[rows:]

    def times(values, halves):
        half = width // 2
        return matmul(values[:, :half], halves[0]) + matmul(values[:, half:], halves[1])

    def times_t(values, halves):
        return jnp.concatenate([matmul_right_t(values, halves[0]), matmul_right_t(values, halves[1])], axis=1)

    in_slice = lax.dynamic_slice_in_dim(in_weight.reshape(own_rows, 3, width), z * part, part, axis=2)
    small = jnp.concatenate([gain_one[:, None], gain_two[:, None], conv_weight.T], axis=1)
    small = jnp.pad(small, ((0, 0), (0, lane - 5)))
    in_slice = jnp.concatenate([in_slice.reshape(own_rows, 3 * part), small], axis=1)
    in_halves = spread_rows(in_slice, direct=True)
    value_all = jnp.concatenate(gather_z(to_rows(tokens_here)), axis=0).astype(f32)
    small = jnp.concatenate([half[:, 3 * part :] for half in in_halves], axis=0)
    gain_rows = small[:, 0].astype(f32)
    small = lax.dot_general(small, order, (((0,), (1,)), ((), ())), preferred_element_type=f32)
    gain_first, gain_second = small[0], small[1]
    taps = lax.dynamic_slice_in_dim(small[2:5], z * part, part, axis=1)
    out_halves = spread_rows(out_weight)
    first_lane = (z * hidden // lane) * lane
    lane_index = jnp.arange(padded, dtype=jnp.int32) - gap * odd
    keep = ((lane_index >= 0) & (lane_index < hidden))[None, :]
    pair_slice = jnp.concatenate(
        [
            jnp.where(keep, lax.dynamic_slice_in_dim(w, first_lane, padded, axis=1), 0).astype(bf16)
            for w in (gate_weight, up_weight)
        ],
        axis=1,
    )
    pair_halves = spread_rows(pair_slice)

    grad_blocks = gather_z(grad_branch)

    down_quarter = lax.dynamic_slice_in_dim(down_weight, ((z - y) % 4) * part, part, axis=1)
    down_quarter = lax.all_gather(down_quarter, "y", axis=0, tiled=False)
    pieces = [
        shift(lax.dynamic_index_in_dim(down_quarter, (z + d) % 4, axis=0, keepdims=False), "z", d) for d in range(4)
    ]
    down_own = jnp.concatenate([pieces[0], pieces[3], pieces[2], pieces[1]], axis=1)
    down_above = shift(down_own[:, : width // 2], ring, 1)
    down_below = shift(down_own[:, width // 2 :], ring, -1)
    down_this = jnp.stack([down_own, jnp.concatenate([down_above, down_below], axis=1)])
    down_other = shift(down_this, "core", 1)
    down_start = [
        gap * odd + hidden_rows * ((xl ^ x) * 2 + (core ^ c)) for c in range(2) for x in range(2)
    ]
    starts = jnp.stack(down_start + [jnp.where(odd == 1, 0, hidden)]).astype(jnp.int32)
    down = place_rows([down_this[0], down_this[1], down_other[0], down_other[1]], starts, padded)

    normed = normalize(value_all, gain_rows)[2]
    base_one, scale_one, _ = normalize(value_here, gain_first)
    triple = times(normed, in_halves).reshape(4, rows, 3 * part + lane)
    input_gate, output_gate, conv_values = (triple[..., i * part : (i + 1) * part] for i in range(3))
    gated_in = input_gate * conv_values
    tails = shift(gated_in[:, rows - 2 :], "xh", 1)
    block_z = (z - jnp.arange(4)) % 4
    first = ((block_z == 0) & (xh == 0))[:, None, None]
    tails = jnp.where(xh == 1, tails, jnp.roll(tails, -1, axis=0))
    tails = jnp.where(first, 0.0, tails)
    extended = jnp.concatenate([tails, gated_in], axis=1)
    conv_out = taps[0] * extended[:, :rows] + taps[1] * extended[:, 1 : rows + 1] + taps[2] * extended[:, 2:]
    mixed = (output_gate * conv_out).astype(bf16)
    mixed = jnp.concatenate([mixed[0]] + [shift(mixed[d], "z", -d) for d in (1, 2, 3)], axis=1)
    mixed = matmul(mixed, channel_order).astype(bf16)
    middle = value_here + times(mixed, out_halves)

    base_two, scale_two, normed_two = normalize(middle, gain_second)
    normed_two = jnp.concatenate(gather_z(to_rows(normed_two)), axis=0)
    grad_all = jnp.concatenate(grad_blocks, axis=0)
    pre = times(normed_two, pair_halves)
    gate_pre, up_pre = pre[:, :padded], pre[:, padded:]
    sigmoid_gate = jax.nn.sigmoid(gate_pre)
    silu_gate = gate_pre * sigmoid_gate
    active = (silu_gate * up_pre).astype(bf16)
    grad_active = matmul_right_t(grad_all, down)
    grad_gate = grad_active * up_pre * sigmoid_gate * (1.0 + gate_pre * (1.0 - sigmoid_gate))
    grad_pair = jnp.concatenate([grad_gate.astype(bf16), (grad_active * silu_gate).astype(bf16)], axis=1)
    grad_normed = times_t(grad_pair, pair_halves).astype(bf16).reshape(4, rows, width)
    grad_normed = from_rows(scatter_z(grad_normed))
    branch = matmul(active, down).astype(bf16).reshape(4, rows, width)
    result = valid * (middle + scatter_z(branch))

    pair_w = combine_rows(normed_two, grad_pair)
    pair_w = lax.all_gather(pair_w, "z", axis=0, tiled=False).astype(f32)

    down_w = matmul_left_t(active, grad_all).astype(bf16)
    down_parts = [lax.dynamic_slice_in_dim(down_w, start, hidden_rows, axis=0) for start in down_start]
    arrived = shift(jnp.stack(down_parts[2:]), "core", 1)
    other_x = (down_parts[1].astype(f32) + arrived[1].astype(f32)).astype(bf16)
    above = shift(other_x[:, : width // 2], ring, 1)
    below = shift(other_x[:, width // 2 :], ring, -1)
    mine = down_parts[0].astype(f32) + arrived[0].astype(f32)
    mine = (mine + jnp.concatenate([above, below], axis=1).astype(f32)).astype(bf16)
    mine = mine.reshape(hidden_rows, 4, part).transpose(1, 0, 2)
    mine = lax.psum_scatter(mine, "y", scatter_dimension=0, tiled=False)
    mine = lax.all_gather(add_partner(mine), "z", axis=0, tiled=False)
    mine = lax.all_to_all(mine, "y", 0, 0, tiled=True)
    grad_down_w = mine.transpose(1, 0, 2).reshape(hidden_rows, width).astype(f32)

    grad_mid_norm = norm_back(grad_normed, base_two, scale_two, gain_second)
    grad_middle = grad_result + grad_mid_norm
    grad_mixer = grad_middle.astype(bf16)

    grad_mixed = times_t(grad_mixer, out_halves).astype(bf16)
    grad_mixed = matmul_right_t(grad_mixed, channel_order).astype(bf16)
    grad_mixed = jnp.stack([shift(grad_mixed[:, d * part : (d + 1) * part], "z", d) for d in range(4)]).astype(f32)
    grad_output_gate = grad_mixed * conv_out
    grad_conv = grad_mixed * output_gate
    heads = shift(grad_conv[:, :2], "xh", 1)
    heads = jnp.where(xh == 0, heads, jnp.roll(heads, 1, axis=0))
    last = ((block_z == 3) & (xh == 1))[:, None, None]
    heads = jnp.where(last, 0.0, heads)
    following = jnp.concatenate([grad_conv, heads], axis=1)
    grad_gated_in = taps[2] * grad_conv + taps[1] * following[:, 1 : rows + 1] + taps[0] * following[:, 2:]
    grad_taps = jnp.stack([jnp.sum(grad_conv * extended[:, k : k + rows], axis=(0, 1)) for k in range(3)])
    grad_triple = jnp.concatenate(
        [
            (grad_gated_in * conv_values).astype(bf16),
            grad_output_gate.astype(bf16),
            (grad_gated_in * input_gate).astype(bf16),
            jnp.zeros((4, rows, lane), bf16),
        ],
        axis=-1,
    ).reshape(4 * rows, 3 * part + lane)
    grad_first = times_t(grad_triple, in_halves).astype(bf16).reshape(4, rows, width)
    grad_first = from_rows(scatter_z(grad_first))
    grad_hidden_norm = norm_back(grad_first, base_one, scale_one, gain_first)
    grad_tokens = grad_middle + grad_hidden_norm

    out_w = combine_rows(mixed, grad_mixer)
    grad_out_w = sum(block.astype(f32) for block in gather_z(out_w))
    tap_rows = lax.dynamic_update_slice(jnp.zeros((lane, width), bf16), grad_taps.astype(bf16), (0, z * part))
    tap_rows = lax.dot_general(order, tap_rows, (((0,), (1,)), ((), ())), preferred_element_type=f32)
    in_w = combine_rows(normed, grad_triple, tap_rows)
    in_w = jnp.stack(in_order(gather_z(in_w), "z")).astype(f32)
    grad_in_w = in_w[..., : 3 * part].reshape(4, own_rows, 3, part).transpose(1, 2, 0, 3).reshape(own_rows, 3 * width)
    grad_conv_w = jnp.sum(in_w[..., 3 * part :], axis=0)[:, :3].T
    grad_gain_one = jnp.sum(grad_in_w * in_weight.astype(f32), axis=1) / gain_one.astype(f32)

    def join(pieces):
        a, b, c, d = (pieces[i] for i in range(4))
        edge = padded - lane
        return jnp.concatenate(
            [
                a[:, :edge], a[:, edge:] + b[:, :lane], b[:, lane:],
                c[:, :edge], c[:, edge:] + d[:, :lane], d[:, lane:],
            ],
            axis=1,
        )

    grad_gate_w = join(pair_w[..., :padded])
    grad_up_w = join(pair_w[..., padded:])

    grad_gain_two = jnp.sum(grad_gate_w * gate_weight.astype(f32) + grad_up_w * up_weight.astype(f32), axis=1)
    grad_gain_two = grad_gain_two / gain_two.astype(f32)

    return (
        result.astype(bf16)[None],
        grad_tokens[None],
        grad_gain_one,
        grad_in_w,
        grad_conv_w,
        grad_out_w,
        grad_gain_two,
        grad_gate_w,
        grad_up_w,
        grad_down_w,
    )


def solution(mesh):
    fine = Mesh(mesh.devices.reshape(4, 2, 4, 2, 2), ("z", "xh", "y", "xl", "core"))
    by_rows = P(owners, None)
    sequences = P(owners, blocks, None)
    return jax.shard_map(
        local,
        mesh=fine,
        in_specs=(
            sequences,
            P(owners),
            sequences,
            P(owners),
            by_rows,
            P(None, owners),
            by_rows,
            P(owners),
            by_rows,
            by_rows,
            by_rows,
        ),
        out_specs=(
            sequences,
            sequences,
            P(owners),
            by_rows,
            P(None, owners),
            by_rows,
            P(owners),
            by_rows,
            by_rows,
            by_rows,
        ),
        check_vma=False,
    )
```

time: 1750 us -> 547 us (0.31)
  waiting for transfers between devices: 1450 us -> 251 us
  blocking collectives: 100 us -> 0 us
  starting transfers between devices: 6.34 us -> 93 us
  matrix products: 140 us -> 93 us
  local copies, waits for them, and re-layouts: 11.7 us -> 50.4 us
    reduce_scatter x5 -> x4, waiting for transfers between devices: 855 us -> 0.08 us  [the longest x3 0.06 us: combine_rows(): mine = lax.psum_scatter(mine, 'y', scatter_dimension=0, tiled=True)]
    all_gather x5, waiting for transfers between devices: 373 us -> 33.4 us  [the longest x2 20.6 us: spread_rows(): own = lax.all_gather(rows, 'y', axis=0, tiled=True)]
    ppermute x2 -> x66, waiting for transfers between devices: 4.61 us -> 217 us  [shift(): lax.ppermute(value, axis, [(i, (i + distance) % size) for i in range(size)])]
    psum x1 -> x0, waiting for transfers between devices: 205 us -> none  [local(): lax.psum(portion_list[1].astype(jnp.bfloat16), 'seq').astype(jnp.float32)]
    ppermute x2 -> x66, starting transfers between devices: 5.61 us -> 89.1 us  [shift(): lax.ppermute(value, axis, [(i, (i + distance) % size) for i in range(size)])]
    unnamed x2 -> x0, blocking collectives: 59.2 us -> none
    dot_general x5 -> x10, matrix products: 53.5 us -> 32.4 us  [matmul_right_t(): lax.dot_general(left, right, (((1,), (1,)), ((), ())), preferred_element_...]
    psum x1 -> x0, blocking collectives: 21 us -> none  [local(): lax.psum(portion_list[0].astype(jnp.bfloat16), 'seq').astype(jnp.float32)]
  transfers between devices with their start and end apart: 14 -> 76, of which waited for: 14 -> 42; matrix products, arithmetic and copies ran while one was open for 6% -> 27% of each run, Pallas kernels for 0% -> 0%
where the time goes in v1:
time: 547 us; the launch traced here: 537 us
  waiting for transfers between devices  251 us (46%)
  starting transfers between devices  93 us (17%)
  matrix products  93 us (17%)
  local copies, waits for them, and re-layouts  50.4 us (9%)
  other arithmetic  31.5 us (6%)
  between operations  16.7 us (3%)
    ppermute x66, waiting for transfers between devices, shift(): lax.ppermute(value, axis, [(i, (i + distance) % size) for i in range(size)])  217 us
    ppermute x66, starting transfers between devices, shift(): lax.ppermute(value, axis, [(i, (i + distance) % size) for i in range(size)])  89.1 us
    dot_general x10, matrix products, matmul_right_t(): lax.dot_general(left, right, (((1,), (1,)), ((), ())), preferred_element_...  32.4 us
    dot_general x10, matrix products, matmul_left_t(): lax.dot_general(left, right, (((0,), (0,)), ((), ())), preferred_element_...  30.4 us
    dot_general x10, matrix products, matmul(): return jnp.dot(left, right, preferred_element_type=f32)  25.6 us
    all_gather x2, waiting for transfers between devices, spread_rows(): own = lax.all_gather(rows, 'y', axis=0, tiled=True)  20.6 us
    unnamed x144, local copies, waits for them, and re-layouts  15.8 us
    all_gather x1, waiting for transfers between devices, local(): pair_w = lax.all_gather(pair_w, 'z', axis=0, tiled=False).astype(f32)  12.7 us
  transfers between devices with their start and end apart: 76, of which 42 were waited for; matrix products, arithmetic and copies ran while one was open for 27% of the time, Pallas kernels for 0%

profile of v1, /device:TPU:1, one launch (start us, length us, event | category | flops | bytes accessed | tf_op | source)
XLA Modules:
  0.0 537.0 jit_solution(8063084946746446046)
XLA Ops:
  13.5 3.6 collective-permute-start.5
  20.0 3.8 collective-permute-start.2
  27.8 8.0 %collective-permute-done.3 = bf16[96,1280]{1,0:T(8,128)(2,1)} collective-permute-done((bf16[96,1280]{1,0:T(8,128)(2,1)S(1)}, bf16[96,1280]{1,0:T(8,128)(2,1)}, u32[]{:S(2)}, u32[]{:S(2)}) %collective-permute-start.3) | collective-permute-done | bytes 245792 | tf_op jit(solution)/shard_map/ppermute | solution.py:22
  44.4 7.6 %collective-permute-done.6 = bf16[192,1280]{1,0:T(8,128)(2,1)S(1)} collective-permute-done((bf16[192,1280]{1,0:T(8,128)(2,1)S(1)}, bf16[192,1280]{1,0:T(8,128)(2,1)S(1)}, u32[]{:S(2)}, u32[]{:S(2)}) %collective-permute-start.6) | collective-permute-done | bytes 491552 | tf_op jit(solution)/shard_map/ppermute | solution.py:22
  59.9 4.5 collective-permute-start.22
  64.4 4.6 all-gather.9.cloned.1.call-done
  82.4 7.1 %collective-permute-done.23 = bf16[432,384]{1,0:T(8,128)(2,1)S(1)} collective-permute-done((bf16[432,384]{1,0:T(8,128)(2,1)S(1)}, bf16[432,384]{1,0:T(8,128)(2,1)S(1)}, u32[]{:S(2)}, u32[]{:S(2)}) %collective-permute-start.23) | collective-permute-done | bytes 331808 | tf_op jit(solution)/shard_map/ppermute | solution.py:22
  93.0 16.1 %all-gather.11.cloned.1.call-done = bf16[384,3584]{1,0:T(8,128)(2,1)} async-done(((bf16[96,3584]{1,0:T(8,128)(2,1)}), bf16[384,3584]{1,0:T(8,128)(2,1)}) %all-gather.11.cloned.1.call-update) | async-done | bytes 2752528 | tf_op jit(solution)/shard_map/all_gather | solution.py:58
  119.4 24.1 %collective-permute-done.19 = bf16[192,3584]{1,0:T(8,128)(2,1)S(1)} collective-permute-done((bf16[192,3584]{1,0:T(8,128)(2,1)S(1)}, bf16[192,3584]{1,0:T(8,128)(2,1)S(1)}, u32[]{:S(2)}, u32[]{:S(2)}) %collective-permute-start.19) | collective-permute-done | bytes 1376288 | tf_op jit(solution)/shard_map/ppermute | solution.py:22
  143.6 5.2 collective-permute-done.20
  150.0 2.7 fusion.79
  152.8 2.7 convolution_add_fusion.4
  183.3 5.4 %collective-permute-done.18 = bf16[128,1536]{1,0:T(8,128)(2,1)S(1)} collective-permute-done((bf16[128,1536]{1,0:T(8,128)(2,1)S(1)}, bf16[128,1536]{1,0:T(8,128)(2,1)S(1)}, u32[]{:S(2)}, u32[]{:S(2)}) %collective-permute-start.18) | collective-permute-done | bytes 393248 | tf_op jit(solution)/shard_map/ppermute | solution.py:22
  188.8 3.6 collective-permute-start.33
  192.5 13.8 %collective-permute-done.16 = bf16[128,1536]{1,0:T(8,128)(2,1)S(1)} collective-permute-done((bf16[128,1536]{1,0:T(8,128)(2,1)S(1)}, bf16[128,1536]{1,0:T(8,128)(2,1)S(1)}, u32[]{:S(2)}, u32[]{:S(2)}) %collective-permute-start.16) | collective-permute-done | bytes 393248 | tf_op jit(solution)/shard_map/ppermute | solution.py:22
  207.7 5.0 fusion.76
  212.7 5.3 convolution_add_fusion
  218.7 3.4 collective-permute-done.31
  222.1 8.7 %multiply_convert_fusion.1 = (bf16[512,1792]{1,0:T(8,128)(2,1)}, bf16[512,1792]{1,0:T(8,128)(2,1)}, bf16[512,1792]{1,0:T(8,128)(2,1)}) fusion(f32[512,3584]{1,0:T(8,128)} %convolution_add_fusion, bf16[1792,1536]{1,0:T(8,128)(2,1)S(1)} %shard_map.186, bf16[128,1536]{1,0:T(8,128)(2,1)S(1)} %collective-permute-done.33, bf16[128,1536]{1,0:T(8,128)(2,1)} %copy-done.58, ...), kind=kOutput, calls=%fused_computation.35 | convolution fusion | flops 2838626304 | bytes 19922944 | tf_op jit(solution)/shard_map/dot_general | solution.py:30
  230.8 5.2 convolution_convert_fusion.7
  236.1 5.0 convolution_convert_fusion.1
  242.0 4.3 convolution_convert_fusion
  247.3 5.6 %convolution_convert_fusion.6 = bf16[512,768]{1,0:T(8,128)(2,1)S(1)} fusion(bf16[768,3584]{1,0:T(8,128)(2,1)} %collective-permute-done.21, bf16[512,1792]{1,0:T(8,128)(2,1)S(1)} %copy-done.61, bf16[512,1792]{1,0:T(8,128)(2,1)S(1)} %copy-done.60), kind=kOutput, calls=%fused_computation.89 | convolution fusion | flops 2826305536 | bytes 9961472 | tf_op jit(solution)/shard_map/dot_general | solution.py:30
  255.7 3.0 convolution_convert_fusion.3
  258.8 14.1 %collective-permute-done.36 = bf16[128,1536]{1,0:T(8,128)(2,1)S(1)} collective-permute-done((bf16[128,1536]{1,0:T(8,128)(2,1)S(1)}, bf16[128,1536]{1,0:T(8,128)(2,1)S(1)}, u32[]{:S(2)}, u32[]{:S(2)}) %collective-permute-start.36) | collective-permute-done | bytes 393248 | tf_op jit(solution)/shard_map/ppermute | solution.py:22
  278.9 2.8 collective-permute-start.64
  281.6 10.2 %collective-permute-done.30 = bf16[128,1536]{1,0:T(8,128)(2,1)S(1)} collective-permute-done((bf16[128,1536]{1,0:T(8,128)(2,1)S(1)}, bf16[128,1536]{1,0:T(8,128)(2,1)S(1)}, u32[]{:S(2)}, u32[]{:S(2)}) %collective-permute-start.30) | collective-permute-done | bytes 393248 | tf_op jit(solution)/shard_map/ppermute | solution.py:22
  294.6 12.6 %collective-permute-done.63 = bf16[432,768]{1,0:T(8,128)(2,1)S(1)} collective-permute-done((bf16[432,768]{1,0:T(8,128)(2,1)S(1)}, bf16[432,768]{1,0:T(8,128)(2,1)S(1)}, u32[]{:S(2)}, u32[]{:S(2)}) %collective-permute-start.63) | collective-permute-done | bytes 663584 | tf_op jit(solution)/shard_map/ppermute | solution.py:22
  309.0 4.7 fusion.11
  334.1 10.2 %collective-permute-done.60 = bf16[192,3584]{1,0:T(8,128)(2,1)} collective-permute-done((bf16[192,3584]{1,0:T(8,128)(2,1)}, bf16[192,3584]{1,0:T(8,128)(2,1)}, u32[]{:S(2)}, u32[]{:S(2)}) %collective-permute-start.60) | collective-permute-done | bytes 1376288 | tf_op jit(solution)/shard_map/ppermute | solution.py:22
  347.0 7.2 %fusion.12 = bf16[384,3584]{1,0:T(8,128)(2,1)} fusion(bf16[768,3584]{1,0:T(8,128)(2,1)} %collective-permute-done.58, bf16[192,3584]{1,0:T(8,128)(2,1)} %collective-permute-done.60, bf16[192,3584]{1,0:T(8,128)(2,1)} %collective-permute-done.59, bf16[512,1536]{1,0:T(8,128)(2,1)} %copy-done.17, bf16[512,1792]{1,0:T(8,128)(2,1)} %get-tuple-element.48, ...), kind=kOutput, calls=%fused_computation.18 | convolution fusion | flops 1427636224 | bytes 12320768 | tf_op jit(solution)/shard_map/dot_general | solution.py:34
  360.1 4.9 collective-permute-start.44
  371.1 10.9 %collective-permute-done.46 = bf16[192,1280]{1,0:T(8,128)(2,1)S(1)} collective-permute-done((bf16[192,1280]{1,0:T(8,128)(2,1)S(1)}, bf16[192,1280]{1,0:T(8,128)(2,1)S(1)}, u32[]{:S(2)}, u32[]{:S(2)}) %collective-permute-start.46) | collective-permute-done | bytes 491552 | tf_op jit(solution)/shard_map/ppermute | solution.py:22
  388.8 12.2 %collective-permute-done.53 = bf16[192,1536]{1,0:T(8,128)(2,1)S(1)} collective-permute-done((bf16[192,1536]{1,0:T(8,128)(2,1)S(1)}, bf16[192,1536]{1,0:T(8,128)(2,1)S(1)}, u32[]{:S(2)}, u32[]{:S(2)}) %collective-permute-start.53) | collective-permute-done | bytes 589856 | tf_op jit(solution)/shard_map/ppermute | solution.py:22
  402.3 2.9 add_convert_fusion
  405.5 2.8 convolution_convert_fusion.5
  408.5 2.8 convolution_convert_fusion.4
  418.9 6.3 %collective-permute-done.43 = bf16[128,1536]{1,0:T(8,128)(2,1)S(1)} collective-permute-done((bf16[128,1536]{1,0:T(8,128)(2,1)}, bf16[128,1536]{1,0:T(8,128)(2,1)S(1)}, u32[]{:S(2)}, u32[]{:S(2)}) %collective-permute-start.43) | collective-permute-done | bytes 393248 | tf_op jit(solution)/shard_map/ppermute | solution.py:22
  427.4 4.8 collective-permute-done.41
  434.4 3.0 collective-permute-start.47
  442.6 4.9 collective-permute-start.50
  451.6 3.0 collective-permute-done.49
  454.6 11.3 %collective-permute-done.48 = bf16[96,1280]{1,0:T(8,128)(2,1)S(1)} collective-permute-done((bf16[96,1280]{1,0:T(8,128)(2,1)S(1)}, bf16[96,1280]{1,0:T(8,128)(2,1)S(1)}, u32[]{:S(2)}, u32[]{:S(2)}) %collective-permute-start.48) | collective-permute-done | bytes 245792 | tf_op jit(solution)/shard_map/ppermute | solution.py:22
  466.2 3.3 collective-permute-start.54
  478.2 3.6 all-to-all-start
  487.1 6.7 %collective-permute-done.57 = bf16[96,1536]{1,0:T(8,128)(2,1)} collective-permute-done((bf16[96,1536]{1,0:T(8,128)(2,1)S(1)}, bf16[96,1536]{1,0:T(8,128)(2,1)}, u32[]{:S(2)}, u32[]{:S(2)}) %collective-permute-start.57) | collective-permute-done | bytes 294944 | tf_op jit(solution)/shard_map/ppermute | solution.py:22
  494.6 11.0 %collective-permute-done.55 = bf16[96,1536]{1,0:T(8,128)(2,1)} collective-permute-done((bf16[96,1536]{1,0:T(8,128)(2,1)S(1)}, bf16[96,1536]{1,0:T(8,128)(2,1)}, u32[]{:S(2)}, u32[]{:S(2)}) %collective-permute-start.55) | collective-permute-done | bytes 294944 | tf_op jit(solution)/shard_map/ppermute | solution.py:22
  509.7 12.7 %all-gather.15.cloned.1.call-done = bf16[384,3584]{1,0:T(8,128)(2,1)} async-done(((bf16[96,3584]{1,0:T(8,128)(2,1)}), bf16[384,3584]{1,0:T(8,128)(2,1)}) %all-gather.15.cloned.1.call-update) | async-done | bytes 2752528 | tf_op jit(solution)/shard_map/all_gather | solution.py:260
  (408 shorter events, 193.3 us)
Async XLA Ops:
  7.2 50.4 %all-gather.13.cloned.1.call-start = ((), (), s32[]{:S(2)}) async-start(), calls=%async_computation.11 | async-start | bytes 1658880 | tf_op jit(solution)/shard_map/all_gather | solution.py:211
  9.3 59.7 %all-gather.9.cloned.1.call-start = ((), (), s32[]{:S(2)}) async-start(), calls=%async_computation.5 | async-start | bytes 1474560 | tf_op jit(solution)/shard_map/all_gather | solution.py:58
  10.0 99.0 %all-gather.11.cloned.1.call-start = ((), (), s32[]{:S(2)}) async-start(), calls=%async_computation.6 | async-start | bytes 3440640 | tf_op jit(solution)/shard_map/all_gather | solution.py:58
  17.5 18.4 %collective-permute-start.3 = (bf16[96,1280]{1,0:T(8,128)(2,1)S(1)}, bf16[96,1280]{1,0:T(8,128)(2,1)}, u32[]{:S(2)}, u32[]{:S(2)}) collective-permute-start(bf16[96,1280]{1,0:T(8,128)(2,1)S(1)} %get-tuple-element.106), channel_id=1, source_target_pairs={{0,4},{4,8},{8,12},{12,0},{1,5},{5,9},{9,13},{13,1},{2,6},{6,10},{... | collective-permute-start | bytes 737288 | tf_op jit(solution)/shard_map/ppermute | solution.py:22
  20.0 22.9 %collective-permute-start.2 = (bf16[128,1536]{1,0:T(8,128)(2,1)S(1)}, bf16[128,1536]{1,0:T(8,128)(2,1)S(1)}, u32[]{:S(2)}, u32[]{:S(2)}) collective-permute-start(bf16[128,1536]{1,0:T(8,128)(2,1)S(1)} %fusion.47), channel_id=1, source_target_pairs={{0,96},{32,0},{64,32},{96,64},{1,97},{33,1},{65,33},{97,65},{2,98}... | collective-permute-start | bytes 1179656 | tf_op jit(solution)/shard_map/ppermute | solution.py:22
  23.8 19.1 %collective-permute-start.1 = (bf16[128,1536]{1,0:T(8,128)(2,1)S(1)}, bf16[128,1536]{1,0:T(8,128)(2,1)S(1)}, u32[]{:S(2)}, u32[]{:S(2)}) collective-permute-start(bf16[128,1536]{1,0:T(8,128)(2,1)S(1)} %fusion.47), channel_id=1, source_target_pairs={{0,64},{32,96},{64,0},{96,32},{1,65},{33,97},{65,1},{97,33},{2,66}... | collective-permute-start | bytes 1179656 | tf_op jit(solution)/shard_map/ppermute | solution.py:22
  26.0 382.3 %reduce-scatter.11.cloned.1.call-start = ((), (), s32[]{:S(2)}) async-start(), calls=%async_computation.10 | async-start | bytes 1658880 | tf_op jit(solution)/shard_map/reduce_scatter | solution.py:271
  27.1 16.9 %collective-permute-start = (bf16[128,1536]{1,0:T(8,128)(2,1)S(1)}, bf16[128,1536]{1,0:T(8,128)(2,1)S(1)}, u32[]{:S(2)}, u32[]{:S(2)}) collective-permute-start(bf16[128,1536]{1,0:T(8,128)(2,1)S(1)} %fusion.47), channel_id=1, source_target_pairs={{0,32},{32,64},{64,96},{96,0},{1,33},{33,65},{65,97},{97,1},{2,34}... | collective-permute-start | bytes 1179656 | tf_op jit(solution)/shard_map/ppermute | solution.py:22
  54.1 61.8 %collective-permute-start.8 = (bf16[768,1280]{1,0:T(8,128)(2,1)}, bf16[768,1280]{1,0:T(8,128)(2,1)}, u32[]{:S(2)}, u32[]{:S(2)}) collective-permute-start(bf16[768,1280]{1,0:T(8,128)(2,1)} %constant_dynamic-update-slice_fusion), channel_id=1, source_target_pairs={{0,1},{1,0},{2,3},{3,2},{4,5},{5,4},{6,7},{7,6},{8,9},{9,8},{10,11... | collective-permute-start | bytes 5898248 | tf_op jit(solution)/shard_map/ppermute | solution.py:22
  59.9 17.7 %collective-permute-start.22 = (bf16[432,384]{1,0:T(8,128)(2,1)}, bf16[432,384]{1,0:T(8,128)(2,1)S(1)}, u32[]{:S(2)}, u32[]{:S(2)}) collective-permute-start(bf16[432,384]{1,0:T(8,128)(2,1)} %get-tuple-element.82), channel_id=1, source_target_pairs={{0,96},{32,0},{64,32},{96,64},{1,97},{33,1},{65,33},{97,65},{2,98}... | collective-permute-start | bytes 995336 | tf_op jit(solution)/shard_map/ppermute | solution.py:22
  71.4 39.8 %collective-permute-start.13 = (bf16[192,1536]{1,0:T(8,128)(2,1)}, bf16[192,1536]{1,0:T(8,128)(2,1)}, u32[]{:S(2)}, u32[]{:S(2)}) collective-permute-start(bf16[192,1536]{1,0:T(8,128)(2,1)} %get-tuple-element.86), channel_id=1, source_target_pairs={{0,2},{2,16},{16,18},{18,0},{1,3},{3,17},{17,19},{19,1},{4,6},{6,2... | collective-permute-start | bytes 1769480 | tf_op jit(solution)/shard_map/ppermute | solution.py:22
  73.9 15.6 %collective-permute-start.23 = (bf16[432,384]{1,0:T(8,128)(2,1)S(1)}, bf16[432,384]{1,0:T(8,128)(2,1)S(1)}, u32[]{:S(2)}, u32[]{:S(2)}) collective-permute-start(bf16[432,384]{1,0:T(8,128)(2,1)S(1)} %copy-done.51), channel_id=1, source_target_pairs={{0,64},{32,96},{64,0},{96,32},{1,65},{33,97},{65,1},{97,33},{2,66}... | collective-permute-start | bytes 995336 | tf_op jit(solution)/shard_map/ppermute | solution.py:22
  77.5 36.1 %collective-permute-start.14 = (bf16[192,1536]{1,0:T(8,128)(2,1)}, bf16[192,1536]{1,0:T(8,128)(2,1)}, u32[]{:S(2)}, u32[]{:S(2)}) collective-permute-start(bf16[192,1536]{1,0:T(8,128)(2,1)} %get-tuple-element.85), channel_id=1, source_target_pairs={{0,18},{2,0},{16,2},{18,16},{1,19},{3,1},{17,3},{19,17},{4,22},{6,... | collective-permute-start | bytes 1769480 | tf_op jit(solution)/shard_map/ppermute | solution.py:22
  81.3 79.2 %collective-permute-start.25 = (bf16[432,768]{1,0:T(8,128)(2,1)}, bf16[432,768]{1,0:T(8,128)(2,1)}, u32[]{:S(2)}, u32[]{:S(2)}) collective-permute-start(bf16[432,768]{1,0:T(8,128)(2,1)} %pad_maximum_fusion.12), channel_id=1, source_target_pairs={{0,2},{2,16},{16,18},{18,0},{1,3},{3,17},{17,19},{19,1},{4,6},{6,2... | collective-permute-start | bytes 1990664 | tf_op jit(solution)/shard_map/ppermute | solution.py:22
  90.4 71.3 %collective-permute-start.26 = (bf16[432,768]{1,0:T(8,128)(2,1)}, bf16[432,768]{1,0:T(8,128)(2,1)}, u32[]{:S(2)}, u32[]{:S(2)}) collective-permute-start(bf16[432,768]{1,0:T(8,128)(2,1)} %pad_maximum_fusion.13), channel_id=1, source_target_pairs={{0,18},{2,0},{16,2},{18,16},{1,19},{3,1},{17,3},{19,17},{4,22},{6,... | collective-permute-start | bytes 1990664 | tf_op jit(solution)/shard_map/ppermute | solution.py:22
  111.2 32.3 %collective-permute-start.19 = (bf16[192,3584]{1,0:T(8,128)(2,1)S(1)}, bf16[192,3584]{1,0:T(8,128)(2,1)S(1)}, u32[]{:S(2)}, u32[]{:S(2)}) collective-permute-start(bf16[192,3584]{1,0:T(8,128)(2,1)S(1)} %get-tuple-element.63), channel_id=1, source_target_pairs={{0,2},{2,16},{16,18},{18,0},{1,3},{3,17},{17,19},{19,1},{4,6},{6,2... | collective-permute-start | bytes 4128776 | tf_op jit(solution)/shard_map/ppermute | solution.py:22
  114.9 61.4 %collective-permute-start.15 = (bf16[768,1536]{1,0:T(8,128)(2,1)S(1)}, bf16[768,1536]{1,0:T(8,128)(2,1)S(1)}, u32[]{:S(2)}, u32[]{:S(2)}) collective-permute-start(bf16[768,1536]{1,0:T(8,128)(2,1)S(1)} %constant_dynamic-update-slice_fusion.6), channel_id=1, source_target_pairs={{0,1},{1,0},{2,3},{3,2},{4,5},{5,4},{6,7},{7,6},{8,9},{9,8},{10,11... | collective-permute-start | bytes 7077896 | tf_op jit(solution)/shard_map/ppermute | solution.py:22
  117.0 31.7 %collective-permute-start.20 = (bf16[192,3584]{1,0:T(8,128)(2,1)S(1)}, bf16[192,3584]{1,0:T(8,128)(2,1)S(1)}, u32[]{:S(2)}, u32[]{:S(2)}) collective-permute-start(bf16[192,3584]{1,0:T(8,128)(2,1)S(1)} %get-tuple-element.62), channel_id=1, source_target_pairs={{0,18},{2,0},{16,2},{18,16},{1,19},{3,1},{17,3},{19,17},{4,22},{6,... | collective-permute-start | bytes 4128776 | tf_op jit(solution)/shard_map/ppermute | solution.py:22
  148.9 58.8 %collective-permute-start.21 = (bf16[768,3584]{1,0:T(8,128)(2,1)S(1)}, bf16[768,3584]{1,0:T(8,128)(2,1)}, u32[]{:S(2)}, u32[]{:S(2)}) collective-permute-start(bf16[768,3584]{1,0:T(8,128)(2,1)S(1)} %constant_dynamic-update-slice_fusion.9), channel_id=1, source_target_pairs={{0,1},{1,0},{2,3},{3,2},{4,5},{5,4},{6,7},{7,6},{8,9},{9,8},{10,11... | collective-permute-start | bytes 16515080 | tf_op jit(solution)/shard_map/ppermute | solution.py:22
  163.0 43.4 %collective-permute-start.27 = (bf16[2,432,1536]{2,1,0:T(8,128)(2,1)S(1)}, bf16[2,432,1536]{2,1,0:T(8,128)(2,1)S(1)}, u32[]{:S(2)}, u32[]{:S(2)}) collective-permute-start(bf16[2,432,1536]{2,1,0:T(8,128)(2,1)S(1)} %pad_maximum_fusion.1), channel_id=1, source_target_pairs={{0,1},{1,0},{2,3},{3,2},{4,5},{5,4},{6,7},{7,6},{8,9},{9,8},{10,11... | collective-permute-start | bytes 7962632 | tf_op jit(solution)/shard_map/ppermute | solution.py:22
  182.5 23.8 %collective-permute-start.16 = (bf16[128,1536]{1,0:T(8,128)(2,1)S(1)}, bf16[128,1536]{1,0:T(8,128)(2,1)S(1)}, u32[]{:S(2)}, u32[]{:S(2)}) collective-permute-start(bf16[128,1536]{1,0:T(8,128)(2,1)S(1)} %fusion.40), channel_id=1, source_target_pairs={{0,32},{32,64},{64,96},{96,0},{1,33},{33,65},{65,97},{97,1},{2,34}... | collective-permute-start | bytes 1179656 | tf_op jit(solution)/shard_map/ppermute | solution.py:22
  188.8 29.2 %collective-permute-start.33 = (bf16[128,1536]{1,0:T(8,128)(2,1)S(1)}, bf16[128,1536]{1,0:T(8,128)(2,1)S(1)}, u32[]{:S(2)}, u32[]{:S(2)}) collective-permute-start(bf16[128,1536]{1,0:T(8,128)(2,1)S(1)} %fusion.74), channel_id=1, source_target_pairs={{0,96},{32,0},{64,32},{96,64},{1,97},{33,1},{65,33},{97,65},{2,98}... | collective-permute-start | bytes 1179656 | tf_op jit(solution)/shard_map/ppermute | solution.py:22
  192.3 25.6 %collective-permute-start.32 = (bf16[128,1536]{1,0:T(8,128)(2,1)S(1)}, bf16[128,1536]{1,0:T(8,128)(2,1)S(1)}, u32[]{:S(2)}, u32[]{:S(2)}) collective-permute-start(bf16[128,1536]{1,0:T(8,128)(2,1)S(1)} %fusion.74), channel_id=1, source_target_pairs={{0,64},{32,96},{64,0},{96,32},{1,65},{33,97},{65,1},{97,33},{2,66}... | collective-permute-start | bytes 1179656 | tf_op jit(solution)/shard_map/ppermute | solution.py:22
  206.3 15.8 %collective-permute-start.31 = (bf16[128,1536]{1,0:T(8,128)(2,1)S(1)}, bf16[128,1536]{1,0:T(8,128)(2,1)}, u32[]{:S(2)}, u32[]{:S(2)}) collective-permute-start(bf16[128,1536]{1,0:T(8,128)(2,1)S(1)} %fusion.74), channel_id=1, source_target_pairs={{0,32},{32,64},{64,96},{96,0},{1,33},{33,65},{65,97},{97,1},{2,34}... | collective-permute-start | bytes 1179656 | tf_op jit(solution)/shard_map/ppermute | solution.py:22
  241.1 68.0 %collective-permute-start.58 = (bf16[768,3584]{1,0:T(8,128)(2,1)}, bf16[768,3584]{1,0:T(8,128)(2,1)}, u32[]{:S(2)}, u32[]{:S(2)}) collective-permute-start(bf16[768,3584]{1,0:T(8,128)(2,1)} %convolution_convert_fusion.1), channel_id=1, source_target_pairs={{0,1},{1,0},{2,3},{3,2},{4,5},{5,4},{6,7},{7,6},{8,9},{9,8},{10,11... | collective-permute-start | bytes 16515080 | tf_op jit(solution)/shard_map/ppermute | solution.py:22
  246.8 31.7 %collective-permute-start.62 = (bf16[2,432,1536]{2,1,0:T(8,128)(2,1)S(1)}, bf16[2,432,1536]{2,1,0:T(8,128)(2,1)S(1)}, u32[]{:S(2)}, u32[]{:S(2)}) collective-permute-start(bf16[2,432,1536]{2,1,0:T(8,128)(2,1)S(1)} %pad_maximum_fusion.2), channel_id=1, source_target_pairs={{0,1},{1,0},{2,3},{3,2},{4,5},{5,4},{6,7},{7,6},{8,9},{9,8},{10,11... | collective-permute-start | bytes 7962632 | tf_op jit(solution)/shard_map/ppermute | solution.py:22
  253.0 19.9 %collective-permute-start.36 = (bf16[128,1536]{1,0:T(8,128)(2,1)S(1)}, bf16[128,1536]{1,0:T(8,128)(2,1)S(1)}, u32[]{:S(2)}, u32[]{:S(2)}) collective-permute-start(bf16[128,1536]{1,0:T(8,128)(2,1)S(1)} %get-tuple-element.70), channel_id=1, source_target_pairs={{0,32},{32,64},{64,96},{96,0},{1,33},{33,65},{65,97},{97,1},{2,34}... | collective-permute-start | bytes 1179656 | tf_op jit(solution)/shard_map/ppermute | solution.py:22
  253.0 19.8 %collective-permute-start.35 = (bf16[128,1536]{1,0:T(8,128)(2,1)S(1)}, bf16[128,1536]{1,0:T(8,128)(2,1)S(1)}, u32[]{:S(2)}, u32[]{:S(2)}) collective-permute-start(bf16[128,1536]{1,0:T(8,128)(2,1)S(1)} %get-tuple-element.71), channel_id=1, source_target_pairs={{0,64},{32,96},{64,0},{96,32},{1,65},{33,97},{65,1},{97,33},{2,66}... | collective-permute-start | bytes 1179656 | tf_op jit(solution)/shard_map/ppermute | solution.py:22
  253.5 20.1 %collective-permute-start.34 = (bf16[128,1536]{1,0:T(8,128)(2,1)S(1)}, bf16[128,1536]{1,0:T(8,128)(2,1)S(1)}, u32[]{:S(2)}, u32[]{:S(2)}) collective-permute-start(bf16[128,1536]{1,0:T(8,128)(2,1)S(1)} %get-tuple-element.69), channel_id=1, source_target_pairs={{0,96},{32,0},{64,32},{96,64},{1,97},{33,1},{65,33},{97,65},{2,98}... | collective-permute-start | bytes 1179656 | tf_op jit(solution)/shard_map/ppermute | solution.py:22
  272.9 18.9 %collective-permute-start.30 = (bf16[128,1536]{1,0:T(8,128)(2,1)S(1)}, bf16[128,1536]{1,0:T(8,128)(2,1)S(1)}, u32[]{:S(2)}, u32[]{:S(2)}) collective-permute-start(bf16[128,1536]{1,0:T(8,128)(2,1)S(1)} %get-tuple-element.73), channel_id=1, source_target_pairs={{0,32},{32,64},{64,96},{96,0},{1,33},{33,65},{65,97},{97,1},{2,34}... | collective-permute-start | bytes 1179656 | tf_op jit(solution)/shard_map/ppermute | solution.py:22
  272.9 20.1 %collective-permute-start.29 = (bf16[128,1536]{1,0:T(8,128)(2,1)S(1)}, bf16[128,1536]{1,0:T(8,128)(2,1)S(1)}, u32[]{:S(2)}, u32[]{:S(2)}) collective-permute-start(bf16[128,1536]{1,0:T(8,128)(2,1)S(1)} %get-tuple-element.74), channel_id=1, source_target_pairs={{0,64},{32,96},{64,0},{96,32},{1,65},{33,97},{65,1},{97,33},{2,66}... | collective-permute-start | bytes 1179656 | tf_op jit(solution)/shard_map/ppermute | solution.py:22
  273.5 19.6 %collective-permute-start.28 = (bf16[128,1536]{1,0:T(8,128)(2,1)S(1)}, bf16[128,1536]{1,0:T(8,128)(2,1)S(1)}, u32[]{:S(2)}, u32[]{:S(2)}) collective-permute-start(bf16[128,1536]{1,0:T(8,128)(2,1)S(1)} %get-tuple-element.72), channel_id=1, source_target_pairs={{0,96},{32,0},{64,32},{96,64},{1,97},{33,1},{65,33},{97,65},{2,98}... | collective-permute-start | bytes 1179656 | tf_op jit(solution)/shard_map/ppermute | solution.py:22
  278.9 15.8 %collective-permute-start.64 = (bf16[432,768]{1,0:T(8,128)(2,1)S(1)}, bf16[432,768]{1,0:T(8,128)(2,1)S(1)}, u32[]{:S(2)}, u32[]{:S(2)}) collective-permute-start(bf16[432,768]{1,0:T(8,128)(2,1)S(1)} %get-tuple-element.76), channel_id=1, source_target_pairs={{0,18},{2,0},{16,2},{18,16},{1,19},{3,1},{17,3},{19,17},{4,22},{6,... | collective-permute-start | bytes 1990664 | tf_op jit(solution)/shard_map/ppermute | solution.py:22
  309.0 109.4 %reduce-scatter.9.cloned.1.call-start = ((), (), s32[]{:S(2)}) async-start(), calls=%async_computation.9 | async-start | bytes 3440640 | tf_op jit(solution)/shard_map/reduce_scatter | solution.py:84
  315.5 28.8 %collective-permute-start.60 = (bf16[192,3584]{1,0:T(8,128)(2,1)}, bf16[192,3584]{1,0:T(8,128)(2,1)}, u32[]{:S(2)}, u32[]{:S(2)}) collective-permute-start(bf16[192,3584]{1,0:T(8,128)(2,1)} %get-tuple-element.61), channel_id=1, source_target_pairs={{0,18},{2,0},{16,2},{18,16},{1,19},{3,1},{17,3},{19,17},{4,22},{6,... | collective-permute-start | bytes 4128776 | tf_op jit(solution)/shard_map/ppermute | solution.py:22
  316.9 30.0 %collective-permute-start.59 = (bf16[192,3584]{1,0:T(8,128)(2,1)}, bf16[192,3584]{1,0:T(8,128)(2,1)}, u32[]{:S(2)}, u32[]{:S(2)}) collective-permute-start(bf16[192,3584]{1,0:T(8,128)(2,1)} %get-tuple-element.60), channel_id=1, source_target_pairs={{0,2},{2,16},{16,18},{18,0},{1,3},{3,17},{17,19},{19,1},{4,6},{6,2... | collective-permute-start | bytes 4128776 | tf_op jit(solution)/shard_map/ppermute | solution.py:22
  329.5 27.3 %collective-permute-start.40 = (f32[4,2,384]{2,1,0:T(2,128)S(1)}, f32[4,2,384]{2,1,0:T(2,128)S(1)}, u32[]{:S(2)}, u32[]{:S(2)}) collective-permute-start(f32[4,2,384]{2,1,0:T(2,128)S(1)} %slice.538), channel_id=1, source_target_pairs={{0,16},{16,0},{1,17},{17,1},{2,18},{18,2},{3,19},{19,3},{4,20},{20... | collective-permute-start | bytes 36872 | tf_op jit(solution)/shard_map/ppermute | solution.py:22
  354.2 80.1 %reduce-scatter.5.cloned.1.call-start = ((), (), s32[]{:S(2)}) async-start(), calls=%async_computation.7 | async-start | bytes 1228800 | tf_op jit(solution)/shard_map/reduce_scatter | solution.py:84
  365.8 19.5 %collective-permute-start.51 = (bf16[768,1536]{1,0:T(8,128)(2,1)S(1)}, bf16[768,1536]{1,0:T(8,128)(2,1)}, u32[]{:S(2)}, u32[]{:S(2)}) collective-permute-start(bf16[768,1536]{1,0:T(8,128)(2,1)S(1)} %convolution_convert_fusion.2), channel_id=1, source_target_pairs={{0,1},{1,0},{2,3},{3,2},{4,5},{5,4},{6,7},{7,6},{8,9},{9,8},{10,11... | collective-permute-start | bytes 7077896 | tf_op jit(solution)/shard_map/ppermute | solution.py:22
  385.3 80.9 %reduce-scatter.7.cloned.1.call-start = ((), (), s32[]{:S(2)}) async-start(), calls=%async_computation.8 | async-start | bytes 1474560 | tf_op jit(solution)/shard_map/reduce_scatter | solution.py:84
  405.3 73.0 %all-gather.17.cloned.1.call-start = ((), (), s32[]{:S(2)}) async-start(), calls=%async_computation.13 | async-start | bytes 1658880 | tf_op jit(solution)/shard_map/all_gather | solution.py:272
  412.3 19.9 %collective-permute-start.41 = (bf16[128,1536]{1,0:T(8,128)(2,1)}, bf16[128,1536]{1,0:T(8,128)(2,1)S(1)}, u32[]{:S(2)}, u32[]{:S(2)}) collective-permute-start(bf16[128,1536]{1,0:T(8,128)(2,1)} %get-tuple-element.66), channel_id=1, source_target_pairs={{0,96},{32,0},{64,32},{96,64},{1,97},{33,1},{65,33},{97,65},{2,98}... | collective-permute-start | bytes 1179656 | tf_op jit(solution)/shard_map/ppermute | solution.py:22
  418.2 104.2 %all-gather.15.cloned.1.call-start = ((), (), s32[]{:S(2)}) async-start(), calls=%async_computation.12 | async-start | bytes 3440640 | tf_op jit(solution)/shard_map/all_gather | solution.py:260
  418.3 19.0 %collective-permute-start.61 = (bf16[96,3584]{1,0:T(8,128)(2,1)}, bf16[96,3584]{1,0:T(8,128)(2,1)}, u32[]{:S(2)}, u32[]{:S(2)}) collective-permute-start(bf16[96,3584]{1,0:T(8,128)(2,1)} %reduce-scatter.9.cloned.1.call-done), channel_id=1, source_target_pairs={{0,16},{16,0},{1,17},{17,1},{2,18},{18,2},{3,19},{19,3},{4,20},{20... | collective-permute-start | bytes 2064392 | tf_op jit(solution)/shard_map/ppermute | solution.py:22
  447.9 18.0 %collective-permute-start.48 = (bf16[96,1280]{1,0:T(8,128)(2,1)S(1)}, bf16[96,1280]{1,0:T(8,128)(2,1)S(1)}, u32[]{:S(2)}, u32[]{:S(2)}) collective-permute-start(bf16[96,1280]{1,0:T(8,128)(2,1)S(1)} %add_convert_fusion.5), channel_id=1, source_target_pairs={{0,32},{32,64},{64,96},{96,0},{1,33},{33,65},{65,97},{97,1},{2,34}... | collective-permute-start | bytes 737288 | tf_op jit(solution)/shard_map/ppermute | solution.py:22
  466.2 15.6 %collective-permute-start.54 = (bf16[96,1536]{1,0:T(8,128)(2,1)}, bf16[96,1536]{1,0:T(8,128)(2,1)}, u32[]{:S(2)}, u32[]{:S(2)}) collective-permute-start(bf16[96,1536]{1,0:T(8,128)(2,1)} %reduce-scatter.7.cloned.1.call-done), channel_id=1, source_target_pairs={{0,16},{16,0},{1,17},{17,1},{2,18},{18,2},{3,19},{19,3},{4,20},{20... | collective-permute-start | bytes 884744 | tf_op jit(solution)/shard_map/ppermute | solution.py:22
  478.2 29.4 %all-to-all-start = ((bf16[4,432,384]{2,1,0:T(8,128)(2,1)}), bf16[4,432,384]{2,1,0:T(8,128)(2,1)S(1)}, u32[]{:S(2)}, u32[]{:S(2)}) async-start(bf16[4,432,384]{2,1,0:T(8,128)(2,1)} %bitcast.170), calls=%async_computation.4 | async-start | bytes 2654208 | tf_op jit(solution)/shard_map/all_to_all | solution.py:273
  483.5 22.1 %collective-permute-start.55 = (bf16[96,1536]{1,0:T(8,128)(2,1)S(1)}, bf16[96,1536]{1,0:T(8,128)(2,1)}, u32[]{:S(2)}, u32[]{:S(2)}) collective-permute-start(bf16[96,1536]{1,0:T(8,128)(2,1)S(1)} %add_convert_fusion.4), channel_id=1, source_target_pairs={{0,32},{32,64},{64,96},{96,0},{1,33},{33,65},{65,97},{97,1},{2,34}... | collective-permute-start | bytes 884744 | tf_op jit(solution)/shard_map/ppermute | solution.py:22
  (92 other events, 817.5 us)
Sparse Core Ops, SparseCore 0:
  10.3 32.5 all-gather.12
  44.5 24.4 all-gather.8
  71.2 37.8 all-gather.10
  309.1 22.3 reduce-scatter.10
  354.3 34.0 reduce-scatter.8
  391.3 21.1 reduce-scatter.4
  415.7 24.2 reduce-scatter.6
  442.3 30.8 all-gather.16
  475.6 46.7 all-gather.14
